TPU v7x, 256 devices: a whole 4x4x8 slice. The times are simulated.
256 devices in a mesh: dev: 256 (over z, y, x, core).
Axes of the slice: x: 4, y: 4, z: 8, core: 2. Of those that a mesh axis runs over, the one named last changes fastest.
Arguments:
- points: float32 [8, 524288], P(None, 'dev'), as said below
- noise: float32 [524288], P('dev'), may hold values from 0.3 to 3
- pattern: int32 [256, 6], P('dev'), may hold values from 0 to 1, as said below
- solution: float32 [16, 524288], P(None, 'dev'), may hold values from -6 to 6
- residual: float32 [16, 524288], P(None, 'dev'), may hold values from -12 to 12
- direction: float32 [16, 524288], P(None, 'dev'), may hold values from -12 to 12
Outputs:
- new_solution: float32 [16, 524288], P(None, 'dev')
- new_residual: float32 [16, 524288], P(None, 'dev')
- new_direction: float32 [16, 524288], P(None, 'dev')
Inputs may be any that keep to these rules, and one draw needn't show every extreme that they name: pattern[i, o - 1] is 1 exactly where some point of block i and some point of block i + o may lie within distance 1 in the first coordinate, 0 where i + o >= 256; some row has a 1 in its last column. points of block i have a first coordinate in an interval that lies after block i - 1's; where pattern[i, o - 1] is 0, and for blocks more than 6 apart, the first coordinates of the two blocks differ by 1 or more; the other coordinates lie in [0, 1).
All inputs are finite; a program needn't handle non-finite values.
Results may differ from a plain program's by a relative error of at most 0.0003.
Values sent between devices are 32-bit elements; how exact they have to be, the bound alone decides.
A program may use at most 64 MiB of HBM per device.

v0:
```python
import functools

import jax
import jax.numpy as jnp
from jax import lax
from jax.experimental import pallas as pl
from jax.experimental.pallas import tpu as pltpu
from jax.sharding import PartitionSpec as P

F = jnp.float32
BF = jnp.bfloat16
MESH = pl.DeviceIdType.MESH
DIMS = 8
RHS = 16
N = 2048
SLOTS = 6
DEVS = 256
DEPTH = 64
C = 256
GROUP = 16
OFFSETS = (1, 2, 3, -4, -5, -6)
VMEM_LIMIT = 48 * 2**20


def split2(x):
    high = x.astype(BF)
    low = (x - high.astype(F)).astype(BF)
    return high.astype(F), low.astype(F)


def split3(x):
    high = x.astype(BF).astype(F)
    rest = x - high
    mid = rest.astype(BF).astype(F)
    low = (rest - mid).astype(BF).astype(F)
    return high, mid, low


def features(points, centre, skip_first):
    row = lax.broadcasted_iota(jnp.int32, points.shape, 0)
    x = jnp.where(row == 0, 0.0 if skip_first else points - centre, points - 0.5)
    norm = jnp.sum(x * x, axis=0, keepdims=True)
    a, b, c = split3(x)
    na, nb, nc = split3(norm)
    ones = jnp.where(row < 3, 1.0, 0.0)
    ones2 = jnp.where((row >= 3) & (row < 6), 1.0, 0.0)
    here = jnp.where(
        row == 0, na, jnp.where(row == 1, nb, jnp.where(row == 2, nc, ones2))
    )
    there = jnp.where(
        row == 3, na, jnp.where(row == 4, nb, jnp.where(row == 5, nc, ones))
    )
    zero = jnp.zeros_like(x)
    left = jnp.concatenate([a, a, b, b, a, c, here, zero], axis=0)
    right = jnp.concatenate(
        [-2.0 * a, -2.0 * b, -2.0 * a, -2.0 * b, -2.0 * c, -2.0 * a, there, zero],
        axis=0,
    )
    return left, right


def kern(dist_sq):
    u = jnp.maximum(dist_sq, 1e-30)
    s = u * lax.rsqrt(u)
    t = jnp.maximum(1.0 - s, 0.0)
    t2 = t * t
    t4 = t2 * t2
    t7 = t4 * (t2 * t)
    return t7 * (8.0 / 7.0 - t)


def halves(v):
    high = v.astype(BF)
    low = (v - high.astype(F)).astype(BF)
    return high, low


def dot(a, b):
    return jnp.dot(a, b, preferred_element_type=F)


def gather_kernel(
    points, noise, direction, got_points, got_dir, image,
    left, right, rows, cols, near, column, send_sem, recv_sem,
):
    me = lax.axis_index("dev")
    barrier = pltpu.get_barrier_semaphore()
    for offset in OFFSETS:
        for signed in (offset, -offset):
            pl.semaphore_signal(
                barrier,
                inc=1,
                device_id=(lax.rem(me + signed + DEVS, DEVS),),
                device_id_type=MESH,
            )
    pl.semaphore_wait(barrier, 2 * SLOTS)
    copies = []
    for slot, offset in enumerate(OFFSETS):
        to = lax.rem(me - offset + DEVS, DEVS)
        for part, (src, dst) in enumerate(
            ((points, got_points.at[slot]), (direction, got_dir.at[slot]))
        ):
            copy = pltpu.make_async_remote_copy(
                src_ref=src,
                dst_ref=dst,
                send_sem=send_sem.at[slot, part],
                recv_sem=recv_sem.at[slot, part],
                device_id=(to,),
                device_id_type=MESH,
            )
            copy.start()
            copies.append(copy)

    a, b = features(points[...], 0.0, True)
    left[...] = a.T.astype(BF)
    right[...] = b.astype(BF)
    both = jnp.concatenate(split2(direction[...] * 7.0), axis=0)
    rows[...] = both.astype(BF)
    cols[...] = both.T.astype(BF)
    first = points[0:1, :]
    column[...] = jnp.broadcast_to(first, (8, N)).T
    near[...] = jnp.zeros_like(near)
    image[...] = noise[...] * direction[...]

    def square(at_row, at_col):
        d = dot(left[at_row, :], right[:, at_col])
        x = column[at_row, 0:1] - points[0:1, at_col]
        high, low = halves(kern(d + x * x))
        w = cols[at_col, :]
        near[at_row, :] += dot(high, w) + dot(low, w)
        return high, low

    def one_column(j, carry):
        at_col = pl.ds(pl.multiple_of(j * C, C), C)

        def one_row(i, acc):
            at_row = pl.ds(pl.multiple_of(i * C, C), C)
            high, low = square(at_row, at_col)
            mine = rows[:, at_row]
            return acc + dot(mine, high) + dot(mine, low)

        far = lax.fori_loop(0, j, one_row, jnp.zeros((2 * RHS, C), F))
        square(at_col, at_col)
        image[:, at_col] += far[:RHS] + far[RHS:]
        return carry

    lax.fori_loop(0, N // C, one_column, 0)
    turned = near[...].T
    image[...] += turned[:RHS] + turned[RHS:]
    for copy in copies:
        copy.wait()


def pair_kernel(
    pattern, points, direction, got_points, got_dir, start, image, far_out,
    left, right, rows, cols, near, column,
):
    first = points[0:1, :]
    least, most = jnp.min(first), jnp.max(first)
    centre = 0.5 * least + 0.5 * most
    both = jnp.concatenate(split2(direction[...] * 7.0), axis=0)
    rows[...] = both.astype(BF)
    near[...] = jnp.zeros_like(near)

    def products(at_row, at_col, dist_sq):
        high, low = halves(kern(dist_sq))
        w = cols[at_col, :]
        near[at_row, :] += dot(high, w) + dot(low, w)
        mine = rows[:, at_row]
        far = dot(mine, high) + dot(mine, low)
        return far[:RHS] + far[RHS:]

    def set_left(skip_first):
        a, _ = features(points[...], centre, skip_first)
        left[...] = a.T.astype(BF)

    set_left(False)
    spread_own = most - least

    def one_slot(slot, carry):
        theirs = got_points[slot, 0:1, :]
        low, high = jnp.min(theirs), jnp.max(theirs)
        own_flag = pattern[0, jnp.minimum(slot, 2)] > 0
        touch = (
            (low - most < 1.0) & (least - high < 1.0) & ((slot > 2) | own_flag)
        )
        reach = jnp.maximum(jnp.maximum(high - centre, centre - low), spread_own)
        narrow = reach <= 1.5

        @pl.when(jnp.logical_not(touch))
        def _():
            far_out[slot] = jnp.zeros((RHS, N), F)

        @pl.when(touch)
        def _():
            vis = jnp.concatenate(split2(got_dir[slot] * 7.0), axis=0)
            cols[...] = vis.T.astype(BF)

        @pl.when(touch & narrow)
        def _():
            _, b = features(got_points[slot], centre, False)
            right[...] = b.astype(BF)

            def one_column(j, c):
                at_col = pl.ds(pl.multiple_of(j * C, C), C)
                d = dot(left[...], right[:, at_col])
                far_out[slot, :, at_col] = products(pl.ds(0, N), at_col, d)
                return c

            lax.fori_loop(0, N // C, one_column, 0)

        @pl.when(touch & jnp.logical_not(narrow))
        def _():
            set_left(True)
            column[...] = jnp.broadcast_to(first, (8, N)).T
            _, b = features(got_points[slot], centre, True)
            right[...] = b.astype(BF)

            def one_column(j, c):
                at_col = pl.ds(pl.multiple_of(j * C, C), C)

                def one_row(i, acc):
                    at_row = pl.ds(pl.multiple_of(i * C, C), C)
                    d = dot(left[at_row, :], right[:, at_col])
                    x = column[at_row, 0:1] - got_points[slot, 0:1, at_col]
                    return acc + products(at_row, at_col, d + x * x)

                far_out[slot, :, at_col] = lax.fori_loop(
                    0, N // C, one_row, jnp.zeros((RHS, C), F)
                )
                return c

            lax.fori_loop(0, N // C, one_column, 0)
            set_left(False)

        return carry

    lax.fori_loop(0, SLOTS, one_slot, 0)
    turned = near[...].T
    image[...] = start[...] + (turned[:RHS] + turned[RHS:])


def finish_kernel(
    partial, far, residual, direction, image, factors,
    got, mine, first_got, second, second_got,
    send_sem, recv_sem, sum_send, sum_recv,
):
    me = lax.axis_index("dev")
    group, place = me // GROUP, lax.rem(me, GROUP)

    def partner(phase, k):
        if phase == 0:
            return group * GROUP + lax.rem(place + k, GROUP)
        return lax.rem(group + k, GROUP) * GROUP + place

    barrier = pltpu.get_barrier_semaphore()
    for offset in OFFSETS:
        for signed in (offset, -offset):
            pl.semaphore_signal(
                barrier,
                inc=1,
                device_id=(lax.rem(me + signed + DEVS, DEVS),),
                device_id_type=MESH,
            )
    for phase in range(2):
        for k in range(1, GROUP):
            pl.semaphore_signal(
                barrier, inc=1, device_id=(partner(phase, k),), device_id_type=MESH
            )
    pl.semaphore_wait(barrier, 2 * SLOTS + 2 * (GROUP - 1))
    copies = []
    for slot, offset in enumerate(OFFSETS):
        copy = pltpu.make_async_remote_copy(
            src_ref=far.at[slot],
            dst_ref=got.at[slot],
            send_sem=send_sem.at[slot],
            recv_sem=recv_sem.at[slot],
            device_id=(lax.rem(me + offset + DEVS, DEVS),),
            device_id_type=MESH,
        )
        copy.start()
        copies.append(copy)
    r, d = residual[...], direction[...]
    rr = jnp.sum(r * r, axis=1, keepdims=True)
    total = partial[...]
    for slot in range(SLOTS):
        copies[slot].wait()
        total = total + got[slot]
    image[...] = total
    curv = jnp.sum(d * total, axis=1, keepdims=True)
    cross = jnp.sum(r * total, axis=1, keepdims=True)
    square = jnp.sum(total * total, axis=1, keepdims=True)
    lane = lax.broadcasted_iota(jnp.int32, (RHS, 128), 1)
    mine[...] = jnp.where(
        lane == 0, rr, jnp.where(lane == 1, curv, jnp.where(lane == 2, cross, square))
    )

    def exchange(phase, source, slots):
        started = []
        for k in range(1, GROUP):
            copy = pltpu.make_async_remote_copy(
                src_ref=source,
                dst_ref=slots.at[k - 1],
                send_sem=sum_send.at[phase, k - 1],
                recv_sem=sum_recv.at[phase, k - 1],
                device_id=(partner(phase, k),),
                device_id_type=MESH,
            )
            copy.start()
            started.append(copy)
        result = source[...]
        for k, copy in enumerate(started):
            copy.wait()
            result = result + slots[k]
        return result

    second[...] = exchange(0, mine, first_got)
    result = exchange(1, second, second_got)
    rr, curv = result[:, 0:1], result[:, 1:2]
    cross, square = result[:, 2:3], result[:, 3:4]
    alpha = rr / curv
    fresh = jnp.maximum(rr - alpha * (2.0 * cross - alpha * square), 0.0)
    beta = fresh / (rr + 1e-05)
    factors[...] = jnp.where(lane == 0, alpha, beta)


def local(points, noise, pattern, solution, residual, direction):
    vmem = pl.BlockSpec(memory_space=pltpu.VMEM)
    hbm = pl.BlockSpec(memory_space=pl.ANY)
    smem = pl.BlockSpec(memory_space=pltpu.SMEM)
    shape = jax.ShapeDtypeStruct
    work = [
        pltpu.VMEM((N, DEPTH), BF),
        pltpu.VMEM((DEPTH, N), BF),
        pltpu.VMEM((2 * RHS, N), BF),
        pltpu.VMEM((N, 2 * RHS), BF),
        pltpu.VMEM((N, 2 * RHS), F),
        pltpu.VMEM((N, 8), F),
    ]
    dma = pltpu.SemaphoreType.DMA
    got_points, got_dir, start = pl.pallas_call(
        gather_kernel,
        out_shape=(
            shape((SLOTS, DIMS, N), F),
            shape((SLOTS, RHS, N), F),
            shape((RHS, N), F),
        ),
        in_specs=[vmem] * 3,
        out_specs=(hbm, hbm, vmem),
        scratch_shapes=[*work, dma((SLOTS, 2)), dma((SLOTS, 2))],
        compiler_params=pltpu.CompilerParams(
            collective_id=0, has_side_effects=True, vmem_limit_bytes=VMEM_LIMIT
        ),
        name="gather_diagonal",
    )(points, noise.reshape(1, N), direction)
    partial, far = pl.pallas_call(
        pair_kernel,
        out_shape=(shape((RHS, N), F), shape((SLOTS, RHS, N), F)),
        in_specs=[smem] + [vmem] * 5,
        out_specs=(vmem, vmem),
        scratch_shapes=work,
        compiler_params=pltpu.CompilerParams(vmem_limit_bytes=VMEM_LIMIT),
        name="pairs",
    )(pattern, points, direction, got_points, got_dir, start)
    image, factors = pl.pallas_call(
        finish_kernel,
        out_shape=(shape((RHS, N), F), shape((RHS, 128), F)),
        in_specs=[vmem] * 4,
        out_specs=(vmem, vmem),
        scratch_shapes=[
            pltpu.VMEM((SLOTS, RHS, N), F),
            pltpu.VMEM((RHS, 128), F),
            pltpu.VMEM((GROUP - 1, RHS, 128), F),
            pltpu.VMEM((RHS, 128), F),
            pltpu.VMEM((GROUP - 1, RHS, 128), F),
            dma((SLOTS,)),
            dma((SLOTS,)),
            dma((2, GROUP - 1)),
            dma((2, GROUP - 1)),
        ],
        compiler_params=pltpu.CompilerParams(
            collective_id=1, has_side_effects=True, vmem_limit_bytes=VMEM_LIMIT
        ),
        name="finish",
    )(partial, far, residual, direction)
    alpha, beta = factors[:, 0:1], factors[:, 1:2]
    new_solution = solution + alpha * direction
    new_residual = residual - alpha * image
    new_direction = new_residual + beta * direction
    return (new_solution, new_residual, new_direction)


def solution(mesh):
    return jax.shard_map(
        local,
        mesh=mesh,
        in_specs=(
            P(None, "dev"),
            P("dev"),
            P("dev", None),
            P(None, "dev"),
            P(None, "dev"),
            P(None, "dev"),
        ),
        out_specs=(P(None, "dev"), P(None, "dev"), P(None, "dev")),
        check_vma=False,
    )
```

profile of v0, /device:TPU:1, one launch (start us, length us, event | category | flops | bytes accessed | tf_op | source)
XLA Modules:
  0.0 120.7 jit_solution(10755815274205342801)
XLA Ops:
  0.6 0.0 copy-start
  0.6 0.9 copy-done
  1.5 0.0 copy-start.3
  1.5 0.8 copy-done.3
  2.4 0.0 copy-start.4
  2.4 0.7 copy-done.4
  3.1 0.0 copy-start.1
  3.1 31.4 %gather_diagonal.1 = (f32[6,8,2048]{2,1,0:T(8,128)S(1)}, f32[6,16,2048]{2,1,0:T(8,128)S(1)}, f32[16,2048]{1,0:T(8,128)S(1)}) custom-call(f32[8,2048]{1,0:T(8,128)S(1)} %copy-done.3, f32[1,2048]{1,0:T(1,128)S(1)} %bitcast.1, f32[16,2048]{1,0:T(8,128)S(1)} %copy-done), custom_call_target="tpu_custom_call" | custom-call | tf_op jit(solution)/shard_map/gather_diagonal/pallas_call | solution.py:341
  34.5 0.0 copy-start.5
  34.5 0.0 copy-done.1
  34.5 0.6 copy-done.5
  35.2 0.0 copy-start.2
  35.2 2.2 %pairs.1 = (f32[16,2048]{1,0:T(8,128)S(1)}, f32[6,16,2048]{2,1,0:T(8,128)S(1)}) custom-call(s32[1,6]{1,0:T(1,128)S(1)} %copy-done.5, f32[8,2048]{1,0:T(8,128)S(1)} %copy-done.3, f32[16,2048]{1,0:T(8,128)S(1)} %copy-done.1, f32[6,8,2048]{2,1,0:T(8,128)S(1)} %get-tuple-element.10.got_points, f32[6,16,2048]{2,1,0:T(8,128)S(1)} %get-tuple-element.11.got_dir, ...), custom_call_target="tpu_custom_call" | custom-call | tf_op jit(solution)/shard_map/pairs/pallas_call | solution.py:356
  37.4 0.0 copy-done.2
  37.4 0.0 copy-start.6
  37.4 82.3 %finish.1 = (f32[16,2048]{1,0:T(8,128)S(1)}, f32[16,128]{1,0:T(8,128)S(1)}) custom-call(f32[16,2048]{1,0:T(8,128)S(1)} %get-tuple-element.13.partial, f32[6,16,2048]{2,1,0:T(8,128)S(1)} %get-tuple-element.14.far, f32[16,2048]{1,0:T(8,128)S(1)} %copy-done.2, f32[16,2048]{1,0:T(8,128)S(1)} %copy-done.1), custom_call_target="tpu_custom_call" | custom-call | tf_op jit(solution)/shard_map/finish/pallas_call | solution.py:365
  119.7 0.2 slice_reduce_fusion
  119.9 0.0 copy-done.6
  119.9 0.8 multiply_add_fusion
Async XLA Ops:
  0.6 0.9 copy-start
  1.5 0.8 copy-start.3
  2.4 0.7 copy-start.4
  3.1 31.4 %copy-start.1 = (f32[16,2048]{1,0:T(8,128)S(1)}, f32[16,2048]{1,0:T(8,128)}, u32[]{:S(2)}) copy-start(f32[16,2048]{1,0:T(8,128)} %direction.5) | copy-start | bytes 393220
  34.5 0.7 copy-start.5
  35.2 2.2 %copy-start.2 = (f32[16,2048]{1,0:T(8,128)S(1)}, f32[16,2048]{1,0:T(8,128)}, u32[]{:S(2)}) copy-start(f32[16,2048]{1,0:T(8,128)} %residual.1) | copy-start | bytes 393220
  37.4 82.5 %copy-start.6 = (f32[16,2048]{1,0:T(8,128)S(1)}, f32[16,2048]{1,0:T(8,128)}, u32[]{:S(2)}) copy-start(f32[16,2048]{1,0:T(8,128)} %param.9) | copy-start | bytes 393220
where the time goes:
time: 121 us
  Pallas kernels  116 us (96%)
  local copies, waits for them, and re-layouts  3.27 us (3%)
    pallas_call x1, Pallas kernels, local(): pl.pallas_call(finish_kernel, out_shape=(shape((RHS, N), F), shape((RHS,...  82.3 us
    pallas_call x1, Pallas kernels, local(): pl.pallas_call(gather_kernel, out_shape=(shape((SLOTS, DIMS, N), F), shap...  31.4 us
    unnamed x14, local copies, waits for them, and re-layouts  3.09 us

commit v1 on v0

v1 whole, which is shorter than its diff:
```python
import jax
import jax.numpy as jnp
from jax import lax
from jax.experimental import pallas as pl
from jax.experimental.pallas import tpu as pltpu
from jax.sharding import PartitionSpec as P

F = jnp.float32
BF = jnp.bfloat16
MESH = pl.DeviceIdType.MESH
DIMS = 8
RHS = 16
N = 2048
DEVS = 256
DEPTH = 64
C = 256
VMEM_LIMIT = 56 * 2**20
AXES = ((1, 2), (2, 4), (8, 4), (32, 8))

SLOTS = 4


def split2(x):
    high = x.astype(BF)
    low = (x - high.astype(F)).astype(BF)
    return high.astype(F), low.astype(F)


def split3(x):
    high = x.astype(BF).astype(F)
    rest = x - high
    mid = rest.astype(BF).astype(F)
    low = (rest - mid).astype(BF).astype(F)
    return high, mid, low


def features(points, centre, skip_first):
    row = lax.broadcasted_iota(jnp.int32, points.shape, 0)
    x = jnp.where(row == 0, 0.0 if skip_first else points - centre, points - 0.5)
    norm = jnp.sum(x * x, axis=0, keepdims=True)
    a, b, c = split3(x)
    na, nb, nc = split3(norm)
    ones = jnp.where(row < 3, 1.0, 0.0)
    ones2 = jnp.where((row >= 3) & (row < 6), 1.0, 0.0)
    here = jnp.where(
        row == 0, na, jnp.where(row == 1, nb, jnp.where(row == 2, nc, ones2))
    )
    there = jnp.where(
        row == 3, na, jnp.where(row == 4, nb, jnp.where(row == 5, nc, ones))
    )
    zero = jnp.zeros_like(x)
    left = jnp.concatenate([a, a, b, b, a, c, here, zero], axis=0)
    right = jnp.concatenate(
        [-2.0 * a, -2.0 * b, -2.0 * a, -2.0 * b, -2.0 * c, -2.0 * a, there, zero],
        axis=0,
    )
    return left, right


def middle(first):
    least = jnp.min(first, axis=1, keepdims=True)
    most = jnp.max(first, axis=1, keepdims=True)
    return 0.5 * least + 0.5 * most


def halves_of_rows(direction):
    return jnp.concatenate(split2(direction * 7.0), axis=0)


def kern(dist_sq):
    u = jnp.minimum(jnp.maximum(dist_sq, 1e-30), 1.0)
    s = u * lax.rsqrt(u)
    t = 1.0 - s
    t2 = t * t
    return ((t2 * t2) * t2) * (t * (8.0 / 7.0 - t))


def halves(v):
    high = v.astype(BF)
    low = (v - high.astype(F)).astype(BF)
    return high, low


def dot(a, b):
    return jnp.dot(a, b, preferred_element_type=F)


def dot_t(a, b):
    return lax.dot_general(a, b, (((1,), (1,)), ((), ())), preferred_element_type=F)


def step(me, by):
    return lax.rem(me + by + DEVS, DEVS)


def visit_routes(me):
    p = lax.rem(me, 2)
    comes_from = (2, 4, -3 - 2 * p, -5 - 2 * p)
    goes_to = (-2, -4, 5 - 2 * p, 7 - 2 * p)
    return p, [step(me, x) for x in comes_from], [step(me, x) for x in goes_to]


def greet(barrier, targets):
    for target in targets:
        pl.semaphore_signal(barrier, inc=1, device_id=(target,), device_id_type=MESH)


def greet_neighbours(barrier, me):
    p, comes_from, goes_to = visit_routes(me)
    greet(barrier, [me + 1 - 2 * p])
    for slot in (0, 2, 3):
        greet(barrier, [comes_from[slot], goes_to[slot]])

    @pl.when(p == 0)
    def _():
        greet(barrier, [comes_from[1], goes_to[1]])

    return 9 - 2 * p


def on_slot(slot, p, act):
    if slot == 1:
        pl.when(p == 0)(act)
    else:
        act()


def gather_kernel(
    points_hbm, noise, direction_hbm,
    got_points, got_dir, other_points, other_dir, left2, rows2, image,
    points, direction, left, right, cols, near, column,
    send_sem, recv_sem, local_sem,
):
    me = lax.axis_index("dev")
    p, comes_from, goes_to = visit_routes(me)
    barrier = pltpu.get_barrier_semaphore()
    count = greet_neighbours(barrier, me)
    load_points = pltpu.make_async_copy(points_hbm, points, local_sem.at[0])
    load_dir = pltpu.make_async_copy(direction_hbm, direction, local_sem.at[1])
    load_points.start()
    load_dir.start()
    pl.semaphore_wait(barrier, count)

    def remote(src, dst, slot, part, to):
        return pltpu.make_async_remote_copy(
            src_ref=src,
            dst_ref=dst,
            send_sem=send_sem.at[slot, part],
            recv_sem=recv_sem.at[slot, part],
            device_id=(to,),
            device_id_type=MESH,
        )

    mate = [
        remote(points_hbm, other_points, SLOTS, 0, me + 1 - 2 * p),
        remote(direction_hbm, other_dir, SLOTS, 1, me + 1 - 2 * p),
    ]
    visits = [
        [
            remote(points_hbm, got_points.at[slot], slot, 0, goes_to[slot]),
            remote(direction_hbm, got_dir.at[slot], slot, 1, goes_to[slot]),
        ]
        for slot in range(SLOTS)
    ]
    for copy in mate:
        copy.start()
    for slot in (2, 3, 1, 0):

        def start(slot=slot):
            for copy in visits[slot]:
                copy.start()

        on_slot(slot, p, start)

    load_points.wait()
    load_dir.wait()
    own = points[...]
    a, b = features(own, 0.0, True)
    left[...] = a.T.astype(BF)
    right[...] = b.astype(BF)
    both = halves_of_rows(direction[...])
    rows2[0] = both.astype(BF)
    cols[...] = both.T.astype(BF)
    column[...] = jnp.broadcast_to(points[0:1, :], (8, N)).T
    near[...] = jnp.zeros_like(near)
    image[...] = noise[...] * direction[...]
    a, _ = features(own, middle(points[0:1, :]), False)
    left2[0] = a.T.astype(BF)

    def square(at_row, at_col):
        d = dot(left[at_row, :], right[:, at_col])
        x = column[at_row, 0:1] - points[0:1, at_col]
        high, low = halves(kern(d + x * x))
        w = cols[at_col, :]
        near[at_row, :] += dot(high, w) + dot(low, w)
        return high, low

    def one_column(j, carry):
        at_col = pl.ds(pl.multiple_of(j * C, C), C)

        def one_row(i, acc):
            at_row = pl.ds(pl.multiple_of(i * C, C), C)
            high, low = square(at_row, at_col)
            mine = rows2[0, :, at_row]
            return acc + dot(mine, high) + dot(mine, low)

        far = lax.fori_loop(0, j, one_row, jnp.zeros((2 * RHS, C), F))
        square(at_col, at_col)
        image[:, at_col] += far[:RHS] + far[RHS:]
        return carry

    lax.fori_loop(0, N // C, one_column, 0)
    turned = near[...].T
    image[...] += turned[:RHS] + turned[RHS:]
    for copy in mate:
        copy.wait()
    a, _ = features(other_points[...], middle(other_points[0:1, :]), False)
    left2[1] = a.T.astype(BF)
    rows2[1] = halves_of_rows(other_dir[...]).astype(BF)
    for slot in range(SLOTS):

        def finish(slot=slot):
            for copy in visits[slot]:
                copy.wait()

        on_slot(slot, p, finish)


def pair_kernel(
    core, pattern, points, got_points, got_dir, other_points, other_dir, left2, rows2,
    start, image, other_image, far_out,
    right, cols, near, near_t, left, column, vis_points, vis_rows,
):
    p = core[0]
    near[...] = jnp.zeros_like(near)
    near_t[...] = jnp.zeros_like(near_t)
    far_out[...] = jnp.zeros_like(far_out)

    def one_pair(k, carry):
        slot, which = k // 2, lax.rem(k, 2)
        met_own = (slot == 0) | ((slot < 3) & (p == 1)) | ((slot == 3) & (p == 0))
        met_other = (slot != 1) | (p == 0)
        own_flag = (slot != 0) | (pattern[0, 1] > 0)
        allowed = ((which == 0) & met_own & own_flag) | ((which == 1) & met_other)

        @pl.when(allowed)
        def _():
            mate = (slot == 1) & (p == 1)
            visitor = jnp.where(mate, other_points[...], got_points[slot])
            host = jnp.where(which == 0, points[...], other_points[...])
            theirs, mine = visitor[0:1, :], host[0:1, :]
            low, high = jnp.min(theirs), jnp.max(theirs)
            least, most = jnp.min(mine), jnp.max(mine)
            centre = middle(mine)
            centre_s = 0.5 * least + 0.5 * most
            touch = (low - most < 1.0) & (least - high < 1.0)
            reach = jnp.maximum(
                jnp.maximum(high - centre_s, centre_s - low), most - least
            )
            narrow = reach <= 1.5

            @pl.when(touch)
            def _():
                vis_points[...] = visitor
                both = halves_of_rows(jnp.where(mate, other_dir[...], got_dir[slot]))
                vis_rows[...] = both.astype(BF)
                cols[...] = both.T.astype(BF)

            @pl.when(touch & narrow)
            def _():
                _, b = features(vis_points[...], centre, False)
                right[...] = b.astype(BF)

                def one_column(j, c):
                    at_col = pl.ds(pl.multiple_of(j * C, C), C)
                    d = dot(left2[which], right[:, at_col])
                    high, low = halves(kern(d))
                    near[which] += dot(high, cols[at_col, :])
                    near_t[which] += dot_t(vis_rows[:, at_col], low)
                    mine = rows2[which]
                    far = dot(mine, high) + dot(mine, low)
                    far_out[slot, :, at_col] += far[:RHS] + far[RHS:]
                    return c

                lax.fori_loop(0, N // C, one_column, 0, unroll=True)

            @pl.when(touch & jnp.logical_not(narrow))
            def _():
                a, _ = features(host, centre, True)
                left[...] = a.T.astype(BF)
                column[...] = jnp.broadcast_to(mine, (8, N)).T
                _, b = features(vis_points[...], centre, True)
                right[...] = b.astype(BF)

                def one_column(j, c):
                    at_col = pl.ds(pl.multiple_of(j * C, C), C)

                    def one_row(i, acc):
                        at_row = pl.ds(pl.multiple_of(i * C, C), C)
                        d = dot(left[at_row, :], right[:, at_col])
                        x = column[at_row, 0:1] - vis_points[0:1, at_col]
                        high, low = halves(kern(d + x * x))
                        w = cols[at_col, :]
                        near[which, at_row, :] += dot(high, w) + dot(low, w)
                        rows = rows2[which, :, at_row]
                        return acc + dot(rows, high) + dot(rows, low)

                    far = lax.fori_loop(
                        0, N // C, one_row, jnp.zeros((2 * RHS, C), F)
                    )
                    far_out[slot, :, at_col] += far[:RHS] + far[RHS:]
                    return c

                lax.fori_loop(0, N // C, one_column, 0)

        return carry

    lax.fori_loop(0, 2 * SLOTS, one_pair, 0)

    def total(which):
        turned = near[which].T + near_t[which]
        return turned[:RHS] + turned[RHS:]

    image[...] = start[...] + total(0)
    other_image[...] = total(1) + jnp.where(p == 1, far_out[1], 0.0)


def finish_kernel(
    partial, other_image, far, residual, direction, image, factors,
    got, sums, sum_got,
    send_sem, recv_sem, sum_send, sum_recv,
):
    me = lax.axis_index("dev")
    p, comes_from, goes_to = visit_routes(me)

    def partner(axis, k):
        stride, size = AXES[axis]
        at = lax.rem(me // stride, size)
        return me + (lax.rem(at + k, size) - at) * stride

    barrier = pltpu.get_barrier_semaphore()
    count = greet_neighbours(barrier, me)
    for axis, (_, size) in enumerate(AXES):
        greet(barrier, [partner(axis, k) for k in range(1, size)])
        count = count + (size - 1)
    pl.semaphore_wait(barrier, count)

    def remote(src, slot, to):
        return pltpu.make_async_remote_copy(
            src_ref=src,
            dst_ref=got.at[slot],
            send_sem=send_sem.at[slot],
            recv_sem=recv_sem.at[slot],
            device_id=(to,),
            device_id_type=MESH,
        )

    returns = [remote(far.at[slot], slot, comes_from[slot]) for slot in range(SLOTS)]
    mate = remote(other_image, SLOTS, me + 1 - 2 * p)
    for slot in (2, 3, 1, 0):
        on_slot(slot, p, returns[slot].start)
    mate.start()
    r, d = residual[...], direction[...]
    rr = jnp.sum(r * r, axis=1, keepdims=True)
    mate.wait()
    image[...] = partial[...] + got[SLOTS]
    for slot in (0, 1, 2, 3):

        def add(slot=slot):
            returns[slot].wait()
            image[...] += got[slot]

        on_slot(slot, p, add)
    total = image[...]
    curv = jnp.sum(d * total, axis=1, keepdims=True)
    cross = jnp.sum(r * total, axis=1, keepdims=True)
    square = jnp.sum(total * total, axis=1, keepdims=True)
    lane = lax.broadcasted_iota(jnp.int32, (RHS, 128), 1)
    sums[0] = jnp.where(
        lane == 0, rr, jnp.where(lane == 1, curv, jnp.where(lane == 2, cross, square))
    )
    at = 0
    for axis, (_, size) in enumerate(AXES):
        started = []
        for k in range(1, size):
            copy = pltpu.make_async_remote_copy(
                src_ref=sums.at[axis],
                dst_ref=sum_got.at[at],
                send_sem=sum_send.at[at],
                recv_sem=sum_recv.at[at],
                device_id=(partner(axis, k),),
                device_id_type=MESH,
            )
            copy.start()
            started.append((copy, at))
            at += 1
        acc = sums[axis]
        for copy, place in started:
            copy.wait()
            acc = acc + sum_got[place]
        sums[axis + 1] = acc
    result = sums[len(AXES)]
    rr, curv = result[:, 0:1], result[:, 1:2]
    cross, square = result[:, 2:3], result[:, 3:4]
    alpha = rr / curv
    fresh = jnp.maximum(rr - alpha * (2.0 * cross - alpha * square), 0.0)
    beta = fresh / (rr + 1e-05)
    factors[...] = jnp.where(lane == 0, alpha, beta)


def local(points, noise, pattern, solution, residual, direction):
    vmem = pl.BlockSpec(memory_space=pltpu.VMEM)
    hbm = pl.BlockSpec(memory_space=pl.ANY)
    smem = pl.BlockSpec(memory_space=pltpu.SMEM)
    shape = jax.ShapeDtypeStruct
    dma = pltpu.SemaphoreType.DMA
    got_points, got_dir, other_points, other_dir, left2, rows2, start = pl.pallas_call(
        gather_kernel,
        out_shape=(
            shape((SLOTS, DIMS, N), F),
            shape((SLOTS, RHS, N), F),
            shape((DIMS, N), F),
            shape((RHS, N), F),
            shape((2, N, DEPTH), BF),
            shape((2, 2 * RHS, N), BF),
            shape((RHS, N), F),
        ),
        in_specs=[hbm, vmem, hbm],
        out_specs=(hbm, hbm, vmem, vmem, vmem, vmem, vmem),
        scratch_shapes=[
            pltpu.VMEM((DIMS, N), F),
            pltpu.VMEM((RHS, N), F),
            pltpu.VMEM((N, DEPTH), BF),
            pltpu.VMEM((DEPTH, N), BF),
            pltpu.VMEM((N, 2 * RHS), BF),
            pltpu.VMEM((N, 2 * RHS), F),
            pltpu.VMEM((N, 8), F),
            dma((SLOTS + 1, 2)),
            dma((SLOTS + 1, 2)),
            dma((2,)),
        ],
        compiler_params=pltpu.CompilerParams(
            collective_id=0, has_side_effects=True, vmem_limit_bytes=VMEM_LIMIT
        ),
        name="gather_diagonal",
    )(points, noise.reshape(1, N), direction)
    core = lax.rem(lax.axis_index("dev"), 2).reshape(1).astype(jnp.int32)
    partial, other_image, far = pl.pallas_call(
        pair_kernel,
        out_shape=(
            shape((RHS, N), F),
            shape((RHS, N), F),
            shape((SLOTS, RHS, N), F),
        ),
        in_specs=[smem] * 2 + [vmem] * 8,
        out_specs=(vmem, vmem, vmem),
        scratch_shapes=[
            pltpu.VMEM((DEPTH, N), BF),
            pltpu.VMEM((N, 2 * RHS), BF),
            pltpu.VMEM((2, N, 2 * RHS), F),
            pltpu.VMEM((2, 2 * RHS, N), F),
            pltpu.VMEM((N, DEPTH), BF),
            pltpu.VMEM((N, 8), F),
            pltpu.VMEM((DIMS, N), F),
            pltpu.VMEM((2 * RHS, N), BF),
        ],
        compiler_params=pltpu.CompilerParams(vmem_limit_bytes=VMEM_LIMIT),
        name="pairs",
    )(
        core, pattern, points, got_points, got_dir, other_points, other_dir, left2,
        rows2, start,
    )
    exchanges = sum(size - 1 for _, size in AXES)
    image, factors = pl.pallas_call(
        finish_kernel,
        out_shape=(shape((RHS, N), F), shape((RHS, 128), F)),
        in_specs=[vmem] * 5,
        out_specs=(vmem, vmem),
        scratch_shapes=[
            pltpu.VMEM((SLOTS + 1, RHS, N), F),
            pltpu.VMEM((len(AXES) + 1, RHS, 128), F),
            pltpu.VMEM((exchanges, RHS, 128), F),
            dma((SLOTS + 1,)),
            dma((SLOTS + 1,)),
            dma((exchanges,)),
            dma((exchanges,)),
        ],
        compiler_params=pltpu.CompilerParams(
            collective_id=1, has_side_effects=True, vmem_limit_bytes=VMEM_LIMIT
        ),
        name="finish",
    )(partial, other_image, far, residual, direction)
    alpha, beta = factors[:, 0:1], factors[:, 1:2]
    new_solution = solution + alpha * direction
    new_residual = residual - alpha * image
    new_direction = new_residual + beta * direction
    return (new_solution, new_residual, new_direction)


def solution(mesh):
    return jax.shard_map(
        local,
        mesh=mesh,
        in_specs=(
            P(None, "dev"),
            P("dev"),
            P("dev", None),
            P(None, "dev"),
            P(None, "dev"),
            P(None, "dev"),
        ),
        out_specs=(P(None, "dev"), P(None, "dev"), P(None, "dev")),
        check_vma=False,
    )
```

time: 121 us -> 102 us (0.84)
  Pallas kernels: 116 us -> 97.5 us
  local copies, waits for them, and re-layouts: 3.27 us -> 0.97 us
    pallas_call x1, Pallas kernels: 82.3 us -> 27.5 us  [local(): pl.pallas_call(finish_kernel, out_shape=(shape((RHS, N), F), shape((RHS,...]
    pallas_call x1, Pallas kernels: 2.19 us -> 39 us  [local(): pl.pallas_call(pair_kernel, out_shape=(shape((RHS, N), F), shape((RHS, N)...]
    unnamed x14 -> x6, local copies, waits for them, and re-layouts: 3.09 us -> 0.01 us
where the time goes in v1:
time: 102 us; the launch traced here: 101 us
  Pallas kernels  97.5 us (96%)
  other arithmetic  1.75 us (2%)
    pallas_call x1, Pallas kernels, local(): pl.pallas_call(pair_kernel, out_shape=(shape((RHS, N), F), shape((RHS, N)...  39 us
    pallas_call x1, Pallas kernels, local(): pl.pallas_call(gather_kernel, out_shape=(shape((SLOTS, DIMS, N), F), shap...  31 us
    pallas_call x1, Pallas kernels, local(): pl.pallas_call(finish_kernel, out_shape=(shape((RHS, N), F), shape((RHS,...  27.5 us

profile of v1, /device:TPU:1, one launch (start us, length us, event | category | flops | bytes accessed | tf_op | source)
XLA Modules:
  0.0 100.9 jit_solution(6229280008715869180)
XLA Ops:
  0.6 31.0 %gather_diagonal.1 = (f32[4,8,2048]{2,1,0:T(8,128)}, f32[4,16,2048]{2,1,0:T(8,128)}, f32[8,2048]{1,0:T(8,128)}, f32[16,2048]{1,0:T(8,128)}, bf16[2,2048,64]{2,1,...) custom-call(f32[8,2048]{1,0:T(8,128)} %points.1, f32[1,2048]{1,0:T(1,128)} %bitcast.2, f32[16,2048]{1,0:T(8,128)} %direction.1), custom_call_target="tpu_custom_call" | custom-call | tf_op jit(solution)/shard_map/gather_diagonal/pallas_call | solution.py:417
  31.7 39.0 %pairs.1 = (f32[16,2048]{1,0:T(8,128)}, f32[16,2048]{1,0:T(8,128)}, f32[4,16,2048]{2,1,0:T(8,128)}) custom-call(s32[1]{0:T(128)} %bitcast.core, s32[1,6]{1,0:T(1,128)} %pattern.1, f32[8,2048]{1,0:T(8,128)} %points.1, f32[4,8,2048]{2,1,0:T(8,128)} %get-tuple-element.15.got_points, f32[4,16,2048]{2,1,0:T(8,128)} %get-tuple-element.16.got_dir, ...), custom_call_target="tpu_custom_call" | custom-call | tf_op jit(solution)/shard_map/pairs/pallas_call | solution.py:448
  70.6 0.0 copy-start
  70.6 0.0 copy-start.1
  70.6 0.0 copy-start.2
  70.6 27.5 %finish.1 = (f32[16,2048]{1,0:T(8,128)}, f32[16,128]{1,0:T(8,128)}) custom-call(f32[16,2048]{1,0:T(8,128)} %get-tuple-element.22.partial, f32[16,2048]{1,0:T(8,128)} %get-tuple-element.23.other_image, f32[4,16,2048]{2,1,0:T(8,128)} %get-tuple-element.24.far, f32[16,2048]{1,0:T(8,128)} %residual.1, f32[16,2048]{1,0:T(8,128)} %direction.1), custom_call_target="tpu_custom_call" | custom-call | tf_op jit(solution)/shard_map/finish/pallas_call | solution.py:474
  98.1 1.0 slice_reduce_fusion
  99.1 0.0 copy-done
  99.1 0.0 copy-done.1
  99.1 0.0 copy-done.2
  99.1 1.7 %multiply_add_fusion = (f32[16,2048]{1,0:T(8,128)}, f32[16,2048]{1,0:T(8,128)}, f32[16,2048]{1,0:T(8,128)}) fusion(f32[16,2048]{1,0:T(8,128)S(1)} %copy-done, f32[16]{0:T(128)S(1)} %get-tuple-element.27, f32[16,2048]{1,0:T(8,128)S(1)} %copy-done.1, f32[16,2048]{1,0:T(8,128)} %get-tuple-element.26, f32[16]{0:T(128)S(1)} %get-tuple-element.28, ...), kind=kLoop, calls=%fused_computation | loop fusion | flops 196608 | bytes 917632 | tf_op jit(solution)/shard_map/add | solution.py:496
Async XLA Ops:
  70.6 28.5 %copy-start = (f32[16,2048]{1,0:T(8,128)S(1)}, f32[16,2048]{1,0:T(8,128)}, u32[]{:S(2)}) copy-start(f32[16,2048]{1,0:T(8,128)} %direction.1) | copy-start | bytes 393220
  70.6 28.5 %copy-start.1 = (f32[16,2048]{1,0:T(8,128)S(1)}, f32[16,2048]{1,0:T(8,128)}, u32[]{:S(2)}) copy-start(f32[16,2048]{1,0:T(8,128)} %residual.1) | copy-start | bytes 393220
  70.6 28.5 %copy-start.2 = (f32[16,2048]{1,0:T(8,128)S(1)}, f32[16,2048]{1,0:T(8,128)}, u32[]{:S(2)}) copy-start(f32[16,2048]{1,0:T(8,128)} %param.9) | copy-start | bytes 393220
